TPU v7x, 32 devices: a whole 2x2x4 slice. The times are simulated.
32 devices in a mesh: dp: 4 (over x, core), fsdp: 8 (over z, y).
Axes of the slice: x: 2, y: 2, z: 4, core: 2. Of those that a mesh axis runs over, the one named last changes fastest.
Arguments:
- block_input: bfloat16 [2, 8192, 2, 1024], P(None, ('dp', 'fsdp')), may hold values from -6 to 6
- out_grad: bfloat16 [2, 8192, 2, 1024], P(None, ('dp', 'fsdp')), may hold values from -6 to 6
- item_lengths: int32 [2, 256], P(None, ('dp', 'fsdp')), may hold values from 8 to 32, as said below
- frame_offsets: int32 [2, 256], P(None, ('dp', 'fsdp')), may hold values from 0 to 24, as said below
- norm_attn: bfloat16 [2, 1024], P(None, 'fsdp'), may hold values from 0.099609375 to 1.8984375
- w_qkv: bfloat16 [2, 1024, 3072], P(None, 'fsdp'), may hold values from -0.1875 to 0.1875
- w_out: bfloat16 [2, 1024, 1024], P(None, 'fsdp'), may hold values from -0.25 to 0.25
- norm_ffn: bfloat16 [2, 1024], P(None, 'fsdp'), may hold values from 0.099609375 to 1.8984375
- w_gate_up: bfloat16 [2, 1024, 5632], P(None, 'fsdp'), may hold values from -0.1875 to 0.1875
- w_down: bfloat16 [2, 2816, 1024], P(None, 'fsdp'), may hold values from -0.109375 to 0.109375
Outputs:
- block_output: bfloat16 [2, 8192, 2, 1024], P(None, ('dp', 'fsdp'))
- input_grad: bfloat16 [2, 8192, 2, 1024], P(None, ('dp', 'fsdp'))
- grad_norm_attn: float32 [2, 1024], P(None, 'fsdp')
- grad_w_qkv: float32 [2, 1024, 3072], P(None, 'fsdp')
- grad_w_out: float32 [2, 1024, 1024], P(None, 'fsdp')
- grad_norm_ffn: float32 [2, 1024], P(None, 'fsdp')
- grad_w_gate_up: float32 [2, 1024, 5632], P(None, 'fsdp')
- grad_w_down: float32 [2, 2816, 1024], P(None, 'fsdp')
Inputs may be any that keep to these rules, and one draw needn't show every extreme that they name: `item_lengths`: the first item of each micro-batch fills all 32 slots; the second holds 8 frames. `frame_offsets`: offset plus length never exceeds 32; the second item of each micro-batch starts at slot 24.
All inputs are finite; a program needn't handle non-finite values.
Results may differ from a plain program's by a relative error of at most 0.013.
Values may be sent and summed in bfloat16 or wider, within the bound.
A program may use at most 448 MiB of HBM per device.

v0:
```python
import math

import jax
import jax.numpy as jnp
from jax import lax
from jax.sharding import PartitionSpec as P

HEADS = 16
FF = 2816
ITEM_SLOTS = 32


EPSILON = 1e-05
PRECISE = lax.Precision.HIGHEST


def shortened(x):

    def short(part):
        return part.astype(jnp.bfloat16) if part.dtype == jnp.float32 else part

    return jax.tree.map(short, x)


def rms_scale(values):
    return lax.rsqrt(jnp.mean(values * values, axis=-1, keepdims=True) + EPSILON)


def matmul(left, right):
    return jnp.dot(left, right, preferred_element_type=jnp.float32)


def contract_rows(left, right):
    return jnp.einsum("fa,fb->ab", left, right, preferred_element_type=jnp.float32)


def times_transposed(left, right):
    return jnp.einsum("fb,ab->fa", left, right, preferred_element_type=jnp.float32)


def norm_backward(values, scale, gain, upstream):
    weighted = gain * upstream
    return scale * weighted - values * scale**3 * jnp.mean(
        values * weighted, axis=-1, keepdims=True
    )


def on_device(
    block_input,
    out_grad,
    item_lengths,
    frame_offsets,
    norm_attn,
    w_qkv,
    w_out,
    norm_ffn,
    w_gate_up,
    w_down,
):
    micro, frames, positions, model_width = block_input.shape
    head_dim = model_width // HEADS
    hidden_size = FF
    head_shape = (frames, positions, HEADS, head_dim)
    slot_index = jnp.arange(ITEM_SLOTS)[None, None, :]
    first_slot = frame_offsets[:, :, None]
    valid_rows = (slot_index >= first_slot) & (slot_index < first_slot + item_lengths[:, :, None])
    valid_rows = valid_rows.astype(jnp.float32).reshape(micro, frames)
    causal = jnp.arange(positions)[:, None] >= jnp.arange(positions)[None, :]
    totals = (
        jnp.zeros((positions, model_width), jnp.float32),
        jnp.zeros((positions, model_width, 3 * model_width), jnp.float32),
        jnp.zeros((positions, model_width, model_width), jnp.float32),
        jnp.zeros((positions, model_width), jnp.float32),
        jnp.zeros((positions, model_width, 2 * hidden_size), jnp.float32),
        jnp.zeros((positions, hidden_size, model_width), jnp.float32),
    )
    output_list = []
    input_grad_list = []
    for batch_index in range(micro):
        inputs = block_input[batch_index].astype(jnp.float32)
        qkv_all, gain_in_all = (
            lax.all_gather(w_qkv, "fsdp", axis=1, tiled=True),
            lax.all_gather(norm_attn, "fsdp", axis=1, tiled=True),
        )
        first_saved = []
        qkv_list = []
        for place in range(positions):
            rows = inputs[:, place]
            scale_one = rms_scale(rows)
            normed = (rows * scale_one * gain_in_all[place]).astype(jnp.bfloat16)
            first_saved.append((scale_one, normed))
            qkv_list.append(matmul(normed, qkv_all[place]).astype(jnp.bfloat16))
        qkv_proj = jnp.stack(qkv_list, axis=1)
        query_heads = qkv_proj[..., :model_width].reshape(head_shape)
        key_heads = qkv_proj[..., model_width : 2 * model_width].reshape(head_shape)
        value_heads = qkv_proj[..., 2 * model_width :].reshape(head_shape)
        scores = jnp.einsum(
            "fihd,fjhd->fhij", query_heads, key_heads, preferred_element_type=jnp.float32
        ) / math.sqrt(head_dim)
        scores = jnp.where(causal, scores, -1e30)
        attention = jax.nn.softmax(scores, axis=-1)
        attention_low = attention.astype(jnp.bfloat16)
        mixed_heads = jnp.einsum(
            "fhij,fjhd->fihd", attention_low, value_heads, preferred_element_type=jnp.float32
        )
        mixed_heads = mixed_heads.reshape(frames, positions, model_width).astype(jnp.bfloat16)
        out_all, gain_two_all, gu_all, down_all = (
            lax.all_gather(w_out, "fsdp", axis=1, tiled=True),
            lax.all_gather(norm_ffn, "fsdp", axis=1, tiled=True),
            lax.all_gather(w_gate_up, "fsdp", axis=1, tiled=True),
            lax.all_gather(w_down, "fsdp", axis=1, tiled=True),
        )
        second_saved = []
        output_rows = []
        for place in range(positions):
            middle = inputs[:, place] + matmul(mixed_heads[:, place], out_all[place])
            scale_two = rms_scale(middle)
            normed_two = (middle * scale_two * gain_two_all[place]).astype(jnp.bfloat16)
            gate_up = matmul(normed_two, gu_all[place])
            hidden = (jax.nn.silu(gate_up[:, :hidden_size]) * gate_up[:, hidden_size:]).astype(
                jnp.bfloat16
            )
            second_saved.append((middle, scale_two, normed_two, gate_up, hidden))
            output_rows.append((middle + matmul(hidden, down_all[place])).astype(jnp.bfloat16))
        output_list.append(jnp.stack(output_rows, axis=1))
        upstream = (
            out_grad[batch_index].astype(jnp.float32) * valid_rows[batch_index][:, None, None]
        )
        out_all, gain_two_all, gu_all, down_all = (
            lax.all_gather(w_out, "fsdp", axis=1, tiled=True),
            lax.all_gather(norm_ffn, "fsdp", axis=1, tiled=True),
            lax.all_gather(w_gate_up, "fsdp", axis=1, tiled=True),
            lax.all_gather(w_down, "fsdp", axis=1, tiled=True),
        )
        out_grads = []
        gain_two_grads = []
        gu_grads = []
        down_grads = []
        middle_grads = []
        attn_grads = []
        for place in range(positions):
            middle, scale_two, normed_two, gate_up, hidden = second_saved[place]
            gate = gate_up[:, :hidden_size]
            up_part = gate_up[:, hidden_size:]
            grad_ffn = upstream[:, place].astype(jnp.bfloat16)
            down_grads.append(contract_rows(hidden, grad_ffn))
            grad_hidden = times_transposed(grad_ffn, down_all[place])
            sigma = jax.nn.sigmoid(gate)
            grad_gate = grad_hidden * up_part * sigma * (1.0 + gate * (1.0 - sigma))
            grad_up = grad_hidden * jax.nn.silu(gate)
            grad_gate_up = jnp.concatenate([grad_gate, grad_up], axis=-1).astype(jnp.bfloat16)
            gu_grads.append(contract_rows(normed_two, grad_gate_up))
            grad_normed_two = times_transposed(grad_gate_up, gu_all[place])
            gain_two_grads.append(jnp.sum(grad_normed_two * middle * scale_two, axis=0))
            grad_middle = upstream[:, place] + norm_backward(
                middle, scale_two, gain_two_all[place], grad_normed_two
            )
            grad_branch = grad_middle.astype(jnp.bfloat16)
            out_grads.append(contract_rows(mixed_heads[:, place], grad_branch))
            attn_grads.append(times_transposed(grad_branch, out_all[place]).astype(jnp.bfloat16))
            middle_grads.append(grad_middle)
        grad_mixed = jnp.stack(attn_grads, axis=1).reshape(head_shape)
        grad_attention = jnp.einsum(
            "fihd,fjhd->fhij", grad_mixed, value_heads, preferred_element_type=jnp.float32
        )
        grad_values = jnp.einsum(
            "fhij,fihd->fjhd", attention_low, grad_mixed, preferred_element_type=jnp.float32
        )
        grad_scores = attention * (
            grad_attention - jnp.sum(attention * grad_attention, axis=-1, keepdims=True)
        )
        grad_scores = grad_scores / math.sqrt(head_dim)
        grad_query = jnp.einsum(
            "fhij,fjhd->fihd", grad_scores, key_heads.astype(jnp.float32), precision=PRECISE
        )
        grad_keys = jnp.einsum(
            "fhij,fihd->fjhd", grad_scores, query_heads.astype(jnp.float32), precision=PRECISE
        )
        flat_shape = (frames, positions, model_width)
        grad_qkv = jnp.concatenate(
            [
                grad_query.reshape(flat_shape),
                grad_keys.reshape(flat_shape),
                grad_values.reshape(flat_shape),
            ],
            axis=-1,
        ).astype(jnp.bfloat16)
        qkv_all, gain_in_all = (
            lax.all_gather(w_qkv, "fsdp", axis=1, tiled=True),
            lax.all_gather(norm_attn, "fsdp", axis=1, tiled=True),
        )
        qkv_grads = []
        gain_one_grads = []
        input_rows = []
        for place in range(positions):
            scale_one, normed = first_saved[place]
            rows = inputs[:, place]
            qkv_grads.append(contract_rows(normed, grad_qkv[:, place]))
            grad_normed = times_transposed(grad_qkv[:, place], qkv_all[place])
            gain_one_grads.append(jnp.sum(grad_normed * rows * scale_one, axis=0))
            input_rows.append(
                (
                    middle_grads[place]
                    + norm_backward(rows, scale_one, gain_in_all[place], grad_normed)
                ).astype(jnp.bfloat16)
            )
        input_grad_list.append(jnp.stack(input_rows, axis=1))
        batch_grads = (
            jnp.stack(gain_one_grads),
            jnp.stack(qkv_grads),
            jnp.stack(out_grads),
            jnp.stack(gain_two_grads),
            jnp.stack(gu_grads),
            jnp.stack(down_grads),
        )
        totals = tuple((total + update for total, update in zip(totals, batch_grads)))
    totals = (
        lax.psum_scatter(totals[0], "fsdp", scatter_dimension=1, tiled=True),
        lax.psum_scatter(totals[1], "fsdp", scatter_dimension=1, tiled=True),
        lax.psum_scatter(totals[2], "fsdp", scatter_dimension=1, tiled=True),
        lax.psum_scatter(totals[3], "fsdp", scatter_dimension=1, tiled=True),
        lax.psum_scatter(totals[4], "fsdp", scatter_dimension=1, tiled=True),
        lax.psum_scatter(totals[5], "fsdp", scatter_dimension=1, tiled=True),
    )
    totals = jax.tree.map(lambda part: part.astype(jnp.float32), lax.psum(shortened(totals), "dp"))
    return (
        jnp.stack(output_list),
        jnp.stack(input_grad_list),
        totals[0],
        totals[1],
        totals[2],
        totals[3],
        totals[4],
        totals[5],
    )


def solution(mesh):
    placed = (
        P(None, ("dp", "fsdp"), None, None),
        P(None, ("dp", "fsdp"), None, None),
        P(None, ("dp", "fsdp")),
        P(None, ("dp", "fsdp")),
        P(None, "fsdp"),
        P(None, "fsdp", None),
        P(None, "fsdp", None),
        P(None, "fsdp"),
        P(None, "fsdp", None),
        P(None, "fsdp", None),
    )
    return jax.shard_map(
        on_device,
        mesh=mesh,
        in_specs=placed,
        out_specs=(
            P(None, ("dp", "fsdp"), None, None),
            P(None, ("dp", "fsdp"), None, None),
            P(None, "fsdp"),
            P(None, "fsdp", None),
            P(None, "fsdp", None),
            P(None, "fsdp"),
            P(None, "fsdp", None),
            P(None, "fsdp", None),
        ),
        check_vma=False,
    )
```

profile of v0, /device:TPU:0, one launch (start us, length us, event | category | flops | bytes accessed | tf_op | source)
XLA Modules:
  0.0 2906.1 jit_solution(17485150779676849928)
XLA Ops:
  10.3 22.4 all_gather.12
  32.7 16.4 all_gather.15
  57.9 131.4 %all-gather.5.cloned.1.call-done = bf16[2,1024,3072]{2,1,0:T(8,128)(2,1)} async-done(((bf16[2,128,3072]{2,1,0:T(8,128)(2,1)}), bf16[2,1024,3072]{2,1,0:T(8,128)(2,1)}) %all-gather.5.cloned.1.call-update) | async-done | bytes 12582928 | tf_op jit(solution)/shard_map/all_gather | solution.py:82
  245.0 17.6 fusion.153
  280.5 18.1 fusion.154
  326.2 377.9 %all-gather.9.cloned.1.call-done = bf16[2,1024,5632]{2,1,0:T(8,128)(2,1)} async-done(((bf16[2,128,5632]{2,1,0:T(8,128)(2,1)}), bf16[2,1024,5632]{2,1,0:T(8,128)(2,1)}) %all-gather.9.cloned.1.call-update) | async-done | bytes 23068688 | tf_op jit(solution)/shard_map/all_gather | solution.py:110
  704.1 10.7 fusion.8
  714.9 154.9 %all-gather.11.cloned.1.call-done = bf16[2,2816,1024]{2,1,0:T(8,128)(2,1)} async-done(((bf16[2,352,1024]{2,1,0:T(8,128)(2,1)}), bf16[2,2816,1024]{2,1,0:T(8,128)(2,1)}) %all-gather.11.cloned.1.call-update) | async-done | bytes 11534352 | tf_op jit(solution)/shard_map/all_gather | solution.py:111
  869.8 9.0 multiply_convert_fusion.1
  878.9 10.1 multiply_reduce_fusion.2
  922.3 10.3 multiply_reduce_fusion.5
  946.7 12.6 bitcast_add_fusion.1
  987.3 17.8 maximum_add_fusion.2
  1045.9 8.7 fusion.38
  1081.8 12.2 multiply_reduce_fusion
  1094.0 20.9 fusion.39
  1120.9 19.0 fusion.40
  1145.9 12.8 multiply_reduce_fusion.1
  1158.7 20.7 fusion.36
  1185.5 19.4 fusion.37
  1232.3 19.0 maximum_add_fusion.1
  1252.5 11.9 convolution_bitcast_fusion.2
  1264.4 10.0 convolution_bitcast_fusion
  1274.5 9.8 convolution_bitcast_fusion.3
  1284.4 9.9 convolution_bitcast_fusion.1
  1294.2 46.4 %maximum_add_fusion = f32[2,1024,5632]{2,1,0:T(8,128)} fusion(f32[1,1024,5632]{2,1,0:T(8,128)} %convolution_bitcast_fusion.2, f32[1,1024,5632]{2,1,0:T(8,128)} %convolution_bitcast_fusion.3, f32[1,1024,5632]{2,1,0:T(8,128)} %convolution_bitcast_fusion, f32[1,1024,5632]{2,1,0:T(8,128)} %convolution_bitcast_fusion.1), kind=kLoop, calls=%fused_computation.2 | loop fusion | flops 34603008 | bytes 138412032 | tf_op jit(solution)/shard_map/add | solution.py:216
  1377.1 117.6 %reduce-scatter.17.cloned.1.call-done = f32[2,352,1024]{2,1,0:T(8,128)} async-done(((f32[2,2816,1024]{2,1,0:T(8,128)}), f32[2,352,1024]{2,1,0:T(8,128)}) %reduce-scatter.17.cloned.1.call-update) | async-done | bytes 2883600 | tf_op jit(solution)/shard_map/reduce_scatter | solution.py:223
  1497.8 404.6 %reduce-scatter.11.cloned.1.call-done = f32[2,128,3072]{2,1,0:T(8,128)} async-done(((f32[2,1024,3072]{2,1,0:T(8,128)}), f32[2,128,3072]{2,1,0:T(8,128)}) %reduce-scatter.11.cloned.1.call-update) | async-done | bytes 3145744 | tf_op jit(solution)/shard_map/reduce_scatter | solution.py:219
  1905.7 728.2 %reduce-scatter.15.cloned.1.call-done = f32[2,128,5632]{2,1,0:T(8,128)} async-done(((f32[2,1024,5632]{2,1,0:T(8,128)}), f32[2,128,5632]{2,1,0:T(8,128)}) %reduce-scatter.15.cloned.1.call-update) | async-done | bytes 5767184 | tf_op jit(solution)/shard_map/reduce_scatter | solution.py:222
  2658.5 39.9 %reduce-scatter.21.cloned.1.call-done = f32[128,2]{1,0:T(8,128)} async-done(((f32[1024,2]{1,0:T(8,128)}), f32[128,2]{1,0:T(8,128)}) %reduce-scatter.21.cloned.1.call-update) | async-done | bytes 1040
  2699.3 63.6 %reduce-scatter.19.cloned.1.call-done = f32[128,2]{1,0:T(8,128)} async-done(((f32[1024,2]{1,0:T(8,128)}), f32[128,2]{1,0:T(8,128)}) %reduce-scatter.19.cloned.1.call-update) | async-done | bytes 1040
  2770.6 116.8 %all-reduce.4.cloned.1.call-done = (bf16[2,128,3072]{2,1,0:T(8,128)(2,1)}, bf16[2,128,1024]{2,1,0:T(8,128)(2,1)}, bf16[2,128,5632]{2,1,0:T(8,128)(2,1)}, bf16[2,352,1024]{2,1,0:T(8,128)(2,1)}) async-done(((bf16[2,128,3072]{2,1,0:T(8,128)(2,1)}, bf16[2,128,1024]{2,1,0:T(8,128)(2,1)}, bf16[2,128,5632]{2,1,0:T(8,128)(2,1)}, bf16[2,352,1024]{2,1,0:T(8,128)(2,1)}), (bf16[2,128,3072]{2,1,0:T(8,128)(2,1)}, ...) | async-done | bytes 6422544 | tf_op jit(solution)/shard_map/psum | solution.py:225
  (417 shorter events, 389.4 us)
Async XLA Ops:
  7.2 25.5 copy-start.123
  7.2 41.9 %copy-start.56 = (bf16[2,256,2,1024]{3,2,1,0:T(2,128)(2,1)S(1)}, bf16[2,256,2,1024]{3,2,1,0:T(2,128)(2,1)}, u32[]{:S(2)}) copy-start(bf16[2,256,2,1024]{3,2,1,0:T(2,128)(2,1)} %param.10) | copy-start | bytes 6291460
  7.2 182.2 %all-gather.5.cloned.1.call-start = ((), (), s32[]{:S(2)}) async-start(), calls=%async_computation.6 | async-start | bytes 14155776 | tf_op jit(solution)/shard_map/all_gather | solution.py:82
  8.0 309.9 %all-gather.7.cloned.1.call-start = ((), (), s32[]{:S(2)}) async-start(), calls=%async_computation.7 | async-start | bytes 4718592 | tf_op jit(solution)/shard_map/all_gather | solution.py:108
  8.7 695.4 %all-gather.9.cloned.1.call-start = ((), (), s32[]{:S(2)}) async-start(), calls=%async_computation.8 | async-start | bytes 25952256 | tf_op jit(solution)/shard_map/all_gather | solution.py:110
  9.4 860.4 %all-gather.11.cloned.1.call-start = ((), (), s32[]{:S(2)}) async-start(), calls=%async_computation.9 | async-start | bytes 12976128 | tf_op jit(solution)/shard_map/all_gather | solution.py:111
  10.0 1365.0 %reduce-scatter.13.cloned.1.call-start = ((), (), s32[]{:S(2)}) async-start(), calls=%async_computation.11 | async-start | bytes 9437184 | tf_op jit(solution)/shard_map/reduce_scatter | solution.py:220
  51.5 269.9 %copy-start = (f32[256,2,1024]{2,0,1:T(8,128)}, f32[256,2,1024]{2,0,1:T(8,128)S(1)}, u32[]{:S(2)}) copy-start(f32[256,2,1024]{2,0,1:T(8,128)S(1)} %fusion.70) | copy-start | bytes 6291460
  52.9 136.5 %copy-start.108 = (f32[256]{0:T(256)}, f32[256]{0:T(256)S(1)}, u32[]{:S(2)}) copy-start(f32[256]{0:T(256)S(1)} %get-tuple-element.109) | copy-start | bytes 3076
  52.9 141.6 %copy-start.110 = (f32[256]{0:T(256)}, f32[256]{0:T(256)S(1)}, u32[]{:S(2)}) copy-start(f32[256]{0:T(256)S(1)} %get-tuple-element.146) | copy-start | bytes 3076
  53.5 163.9 %copy-start.104 = (f32[256]{0:T(256)}, f32[256]{0:T(256)S(1)}, u32[]{:S(2)}) copy-start(f32[256]{0:T(256)S(1)} %get-tuple-element.117) | copy-start | bytes 3076
  53.5 168.5 %copy-start.106 = (f32[256]{0:T(256)}, f32[256]{0:T(256)S(1)}, u32[]{:S(2)}) copy-start(f32[256]{0:T(256)S(1)} %get-tuple-element.142) | copy-start | bytes 3076
  53.5 908.9 %copy-start.77 = (f32[1,1024]{1,0:T(1,128)}, f32[1,1024]{1,0:T(1,128)S(1)}, u32[]{:S(2)}) copy-start(f32[1,1024]{1,0:T(1,128)S(1)} %get-tuple-element.102) | copy-start | bytes 12292
  53.5 908.9 %copy-start.79 = (f32[1,1024]{1,0:T(1,128)}, f32[1,1024]{1,0:T(1,128)S(1)}, u32[]{:S(2)}) copy-start(f32[1,1024]{1,0:T(1,128)S(1)} %get-tuple-element.103) | copy-start | bytes 12292
  54.0 163.3 %copy-start.92 = (f32[1,1024]{1,0:T(1,128)}, f32[1,1024]{1,0:T(1,128)S(1)}, u32[]{:S(2)}) copy-start(f32[1,1024]{1,0:T(1,128)S(1)} %get-tuple-element.104) | copy-start | bytes 12292
  54.0 168.0 %copy-start.94 = (f32[1,1024]{1,0:T(1,128)}, f32[1,1024]{1,0:T(1,128)S(1)}, u32[]{:S(2)}) copy-start(f32[1,1024]{1,0:T(1,128)S(1)} %get-tuple-element.105) | copy-start | bytes 12292
  280.5 40.9 %copy-start.27 = (bf16[256,2,16,64]{0,3,2,1:T(8,128)(2,1)}, bf16[256,2,16,64]{0,3,2,1:T(8,128)(2,1)S(1)}, u32[]{:S(2)}) copy-start(bf16[256,2,16,64]{0,3,2,1:T(8,128)(2,1)S(1)} %copy.115) | copy-start | bytes 3145732
  321.4 625.3 %copy-start.102 = (f32[256]{0:T(256)}, f32[256]{0:T(256)S(1)}, u32[]{:S(2)}) copy-start(f32[256]{0:T(256)S(1)} %get-tuple-element.121) | copy-start | bytes 3076
  323.1 623.6 %copy-start.100 = (f32[256]{0:T(256)}, f32[256]{0:T(256)S(1)}, u32[]{:S(2)}) copy-start(f32[256]{0:T(256)S(1)} %get-tuple-element.119) | copy-start | bytes 3076
  324.4 638.0 %copy-start.14 = (f32[256,1024]{1,0:T(8,128)}, f32[256,1024]{1,0:T(8,128)S(1)}, u32[]{:S(2)}) copy-start(f32[256,1024]{1,0:T(8,128)S(1)} %get-tuple-element.131) | copy-start | bytes 3145732
  324.4 638.0 %copy-start.98 = (f32[256]{0:T(256)}, f32[256]{0:T(256)S(1)}, u32[]{:S(2)}) copy-start(f32[256]{0:T(256)S(1)} %get-tuple-element.113) | copy-start | bytes 3076
  326.2 636.2 %copy-start.96 = (f32[256]{0:T(256)}, f32[256]{0:T(256)S(1)}, u32[]{:S(2)}) copy-start(f32[256]{0:T(256)S(1)} %get-tuple-element.111) | copy-start | bytes 3076
  704.1 165.7 %copy-start.29 = (f32[256,2,1024]{2,0,1:T(8,128)S(1)}, f32[256,2,1024]{2,0,1:T(8,128)}, u32[]{:S(2)}) copy-start(f32[256,2,1024]{2,0,1:T(8,128)} %get-tuple-element.144) | copy-start | bytes 6291460
  909.1 13.2 copy-start.124
  970.5 524.2 %reduce-scatter.17.cloned.1.call-start = ((), (), s32[]{:S(2)}) async-start(), calls=%async_computation.13 | async-start | bytes 25952256 | tf_op jit(solution)/shard_map/reduce_scatter | solution.py:223
  1005.2 897.3 %reduce-scatter.11.cloned.1.call-start = ((), (), s32[]{:S(2)}) async-start(), calls=%async_computation.10 | async-start | bytes 28311552 | tf_op jit(solution)/shard_map/reduce_scatter | solution.py:219
  1251.3 13.1 copy-start.103
  1251.3 1382.6 %reduce-scatter.15.cloned.1.call-start = ((), (), s32[]{:S(2)}) async-start(), calls=%async_computation.12 | async-start | bytes 51904512 | tf_op jit(solution)/shard_map/reduce_scatter | solution.py:222
  1340.7 1357.6 %reduce-scatter.21.cloned.1.call-start = ((), (), s32[]{:S(2)}) async-start(), calls=%async_computation.15 | async-start | bytes 589824
  1342.5 1420.4 %reduce-scatter.19.cloned.1.call-start = ((), (), s32[]{:S(2)}) async-start(), calls=%async_computation.14 | async-start | bytes 589824
  1342.7 15.8 slice-start
  1363.4 1524.0 %all-reduce.4.cloned.1.call-start = ((), (), s32[]{:S(2)}) async-start(), calls=%async_computation.16 | async-start | bytes 12845056 | tf_op jit(solution)/shard_map/psum | solution.py:225
  (107 other events, 533.1 us)
Sparse Core Ops, SparseCore 0:
  10.2 179.0 all-gather.4
  191.6 71.5 all-gather.6
  264.7 439.3 all-gather.8
  706.2 163.6 all-gather.10
  970.6 147.2 reduce-scatter.12
  1122.1 372.5 reduce-scatter.16
  1499.1 403.3 reduce-scatter.10
  1906.8 727.0 reduce-scatter.14
  2637.3 61.0 reduce-scatter.20
  2701.9 60.9 reduce-scatter.18
  2766.1 121.2 all-reduce.3
where the time goes:
time: 2920 us; the launch traced here: 2910 us
  waiting for transfers between devices  2140 us (73%)
  matrix products  428 us (15%)
  other arithmetic  151 us (5%)
  local copies, waits for them, and re-layouts  128 us (4%)
  blocking collectives  44.4 us (2%)
    reduce_scatter x1, waiting for transfers between devices, on_device(): lax.psum_scatter(totals[4], 'fsdp', scatter_dimension=1, tiled=True)  728 us
    reduce_scatter x1, waiting for transfers between devices, on_device(): lax.psum_scatter(totals[1], 'fsdp', scatter_dimension=1, tiled=True)  405 us
    all_gather x1, waiting for transfers between devices, on_device(): lax.all_gather(w_gate_up, 'fsdp', axis=1, tiled=True)  378 us
    all_gather x1, waiting for transfers between devices, on_device(): lax.all_gather(w_down, 'fsdp', axis=1, tiled=True)  155 us
    all_gather x1, waiting for transfers between devices, on_device(): lax.all_gather(w_qkv, 'fsdp', axis=1, tiled=True)  131 us
    reduce_scatter x1, waiting for transfers between devices, on_device(): lax.psum_scatter(totals[5], 'fsdp', scatter_dimension=1, tiled=True)  118 us
    psum x1, waiting for transfers between devices, on_device(): lax.psum(shortened(totals), 'dp')  117 us
    unnamed x13, waiting for transfers between devices  106 us
  transfers between devices with their start and end apart: 11, of which 9 were waited for; matrix products, arithmetic and copies ran while one was open for 20% of the time, Pallas kernels for 0%

commit v1 on v0

--- a/solution.py
+++ b/solution.py
@@ -1,17 +1,413 @@
+import functools
 import math
 
 import jax
 import jax.numpy as jnp
 from jax import lax
+from jax.experimental import pallas as pl
+from jax.experimental.pallas import tpu as pltpu
 from jax.sharding import PartitionSpec as P
 
+MESH = pl.DeviceIdType.MESH
+BF = jnp.bfloat16
+F32 = jnp.float32
 HEADS = 16
-FF = 2816
 ITEM_SLOTS = 32
-
-
 EPSILON = 1e-05
-PRECISE = lax.Precision.HIGHEST
+LANES = 3
+AXES = ("dp", "fsdp")
+
+
+def place(n):
+    dp, f = lax.axis_index("dp"), lax.axis_index("fsdp")
+    x, c = lax.div(dp, 2), lax.rem(dp, 2)
+    z, h = lax.div(f, 2), lax.rem(f, 2)
+    r = z * (1 - h) + (n - 1 - z) * h
+    return x, c, f, r
+
+
+def ring_index(r, n):
+    hh = lax.div(r, n // 2)
+    return (2 * r) * (1 - hh) + (2 * (n - 1 - r) + 1) * hh
+
+
+class Spot:
+    def __init__(self, n):
+        self.n = n
+        x, c, f, r = place(n)
+        self.x, self.c, self.f, self.r = x, c, f, r
+        self.d = 1 - 2 * c
+        dp = 2 * x + c
+        self.next = (dp, ring_index(lax.rem(r + self.d + n, n), n))
+        self.prev = (dp, ring_index(lax.rem(r - self.d + n, n), n))
+        self.sib = (2 * x + 1 - c, f)
+        self.mate = (2 * (1 - x) + c, f)
+
+    def owner(self, hop):
+        return ring_index(lax.rem(self.r - self.d * (hop + 1) + self.n, self.n), self.n)
+
+    def greet(self):
+        barrier = pltpu.get_barrier_semaphore()
+        for who in (self.next, self.prev, self.sib, self.mate):
+            pl.semaphore_signal(barrier, inc=1, device_id=who, device_id_type=MESH)
+        pl.semaphore_wait(barrier, 4)
+
+
+def remote(src, dst, send, recv, who):
+    return pltpu.make_async_remote_copy(src, dst, send, recv, device_id=who, device_id_type=MESH)
+
+
+def cut(rows, parts):
+    while parts > 1 and rows % (16 * parts):
+        parts -= 1
+    return parts
+
+
+def pieces_of(shapes, parts):
+    out = []
+    for a, (shape, count) in enumerate(zip(shapes, parts)):
+        count = cut(shape[0], count)
+        rows = shape[0] // count
+        for k in range(count):
+            out.append((a, k * rows, rows, shape[1] // 2))
+    return out
+
+
+def lanes_of(pieces):
+    return [pieces[k::LANES] for k in range(LANES)]
+
+
+def gather_kernel(n, lanes, shard_rows, *refs):
+    xs, xo, gs, go, wq, wo, wg, wd = refs[:8]
+    xr, gr, aq, ao, ag, ad = refs[8:14]
+    ring_send, ring_recv, sib_send, sib_recv, loc, swap_send, swap_recv = refs[14:]
+    spot = Spot(n)
+    shards, wholes = (wq, wo, wg, wd), (aq, ao, ag, ad)
+    half = xo.shape[0]
+    local = []
+    for k, (src, dst, count) in enumerate(zip(shards, wholes, shard_rows)):
+        cp = pltpu.make_async_copy(src.at[spot.x], dst.at[pl.ds(spot.f * count, count)], loc.at[k])
+        cp.start()
+        local.append(cp)
+    for k, (src, dst) in enumerate(((xo, xr), (go, gr))):
+        cp = pltpu.make_async_copy(src, dst.at[pl.ds(spot.x * half, half)], loc.at[4 + k])
+        cp.start()
+        local.append(cp)
+    spot.greet()
+    swaps = []
+    for k, (src, dst) in enumerate(((xs, xr), (gs, gr))):
+        cp = remote(src, dst.at[pl.ds(spot.x * half, half)], swap_send.at[k], swap_recv.at[k], spot.mate)
+        cp.start()
+        swaps.append(cp)
+
+    def block(piece, owner):
+        a, first, rows, cols = piece
+        return wholes[a].at[pl.ds(owner * shard_rows[a] + first, rows), pl.ds(spot.c * cols, cols)]
+
+    def send(lane, t):
+        piece, hop = lanes[lane][t // (n - 1)], t % (n - 1)
+        a, first, rows, cols = piece
+        if hop == 0:
+            src = shards[a].at[spot.x, pl.ds(first, rows), pl.ds(spot.c * cols, cols)]
+            dst = block(piece, spot.f)
+        else:
+            src = dst = block(piece, spot.owner(hop - 1))
+        cp = remote(src, dst, ring_send.at[lane, t], ring_recv.at[lane, t], spot.next)
+        cp.start()
+        return cp
+
+    total = [len(lane) * (n - 1) for lane in lanes]
+    flying = {lane: send(lane, 0) for lane in range(len(lanes)) if total[lane]}
+    done = list(swaps)
+    sent = []
+    for t in range(max(total)):
+        for lane in range(len(lanes)):
+            if t >= total[lane]:
+                continue
+            flying[lane].wait_recv()
+            sent.append(flying[lane])
+            if t + 1 < total[lane]:
+                flying[lane] = send(lane, t + 1)
+            piece, hop = lanes[lane][t // (n - 1)], t % (n - 1)
+            arrived = block(piece, spot.owner(hop))
+            cp = remote(arrived, arrived, sib_send.at[lane, t], sib_recv.at[lane, t], spot.sib)
+            cp.start()
+            done.append(cp)
+    for cp in local:
+        cp.wait()
+    for cp in sent:
+        cp.wait_send()
+    for cp in done:
+        cp.wait()
+
+
+def gather(n, xs, xo, gs, go, wq, wo, wg, wd):
+    weights = (wq, wo, wg, wd)
+    shapes = [w.shape[1:] for w in weights]
+    lanes = lanes_of(pieces_of(shapes, (2, 1, 4, 2)))
+    steps = max(len(lane) for lane in lanes) * (n - 1)
+    rows = xo.shape[0]
+    hbm = pl.BlockSpec(memory_space=pltpu.HBM)
+    out = [jax.ShapeDtypeStruct((2 * rows, xo.shape[1]), BF)] * 2 + [
+        jax.ShapeDtypeStruct((s[0] * n, s[1]), BF) for s in shapes
+    ]
+    return pl.pallas_call(
+        functools.partial(gather_kernel, n, lanes, [s[0] for s in shapes]),
+        out_shape=out,
+        in_specs=[hbm] * 8,
+        out_specs=[hbm] * 6,
+        scratch_shapes=[pltpu.SemaphoreType.DMA((LANES, steps))] * 4
+        + [pltpu.SemaphoreType.DMA((6,)), pltpu.SemaphoreType.DMA((2,)), pltpu.SemaphoreType.DMA((2,))],
+        compiler_params=pltpu.CompilerParams(collective_id=0, has_side_effects=True),
+        name="gather_weights",
+    )(xs, xo, gs, go, *weights)
+
+
+def scatter_kernel(n, lanes, shard_rows, *refs):
+    mine = refs[:4]
+    outs = refs[4:8]
+    arrived, ends = refs[8:12], refs[12:16]
+    ring_send, ring_recv, loc, sib_send, sib_recv, mate_send, mate_recv, far_send, far_recv = refs[16:]
+    spot = Spot(n)
+    spot.greet()
+
+    def own(piece, owner):
+        a, first, rows, cols = piece
+        return mine[a].at[pl.ds(owner * shard_rows[a] + first, rows), :]
+
+    def landing(piece, hop):
+        a, first, rows, cols = piece
+        return arrived[a].at[first // rows * (n - 1) + hop]
+
+    total = [len(lane) * (n - 1) for lane in lanes]
+    flying = {}
+    sent = []
+    tail = []
+
+    def launch(lane, t):
+        piece, hop = lanes[lane][t // (n - 1)], t % (n - 1)
+        src = own(piece, spot.owner(hop))
+        if hop:
+            held = landing(piece, hop - 1)
+            held[...] = (held[...].astype(F32) + src[...].astype(F32)).astype(BF)
+            src = held
+        cp = remote(src, landing(piece, hop), ring_send.at[lane, t], ring_recv.at[lane, t], spot.next)
+        cp.start()
+        flying[lane] = cp
+
+    for lane in range(len(lanes)):
+        if total[lane]:
+            launch(lane, 0)
+    mates = []
+    k = 0
+    for t in range(max(total)):
+        for lane in range(len(lanes)):
+            if t >= total[lane]:
+                continue
+            flying[lane].wait_recv()
+            sent.append(flying[lane])
+            piece, hop = lanes[lane][t // (n - 1)], t % (n - 1)
+            if t + 1 < total[lane]:
+                launch(lane, t + 1)
+            if hop < n - 2:
+                continue
+            a, first, rows, cols = piece
+            end = ends[a].at[pl.ds(first, rows), :]
+            end[...] = (own(piece, spot.f)[...].astype(F32) + landing(piece, hop)[...].astype(F32)).astype(BF)
+            spread = outs[a].at[spot.x, pl.ds(first, rows), pl.ds(spot.c * cols, cols)]
+            cp = pltpu.make_async_copy(end, spread, loc.at[k])
+            cp.start()
+            tail.append(cp)
+            cp = remote(end, spread, sib_send.at[k], sib_recv.at[k], spot.sib)
+            cp.start()
+            tail.append(cp)
+            cp = remote(end, spread, mate_send.at[k], mate_recv.at[k], spot.mate)
+            cp.start()
+            mates.append((cp, piece, k))
+            k += 1
+    for cp, piece, k in mates:
+        cp.wait()
+        a, first, rows, cols = piece
+        other = outs[a].at[1 - spot.x, pl.ds(first, rows), pl.ds(spot.c * cols, cols)]
+        far = remote(other, other, far_send.at[k], far_recv.at[k], spot.sib)
+        far.start()
+        tail.append(far)
+    for cp in tail:
+        cp.wait()
+    for cp in sent:
+        cp.wait_send()
+
+
+def scatter(n, grads):
+    shapes = [(g.shape[0] // n, 2 * g.shape[1]) for g in grads]
+    pieces = pieces_of(shapes, (2, 1, 4, 2))
+    lanes = lanes_of(pieces[::-1])
+    steps = max(len(lane) for lane in lanes) * (n - 1)
+    vmem = pl.BlockSpec(memory_space=pltpu.VMEM)
+    dma = pltpu.SemaphoreType.DMA
+    count = len(pieces)
+    landings = []
+    for a in range(4):
+        part = [p for p in pieces if p[0] == a]
+        landings.append(pltpu.VMEM((len(part) * (n - 1), part[0][2], part[0][3]), BF))
+    return pl.pallas_call(
+        functools.partial(scatter_kernel, n, lanes, [s[0] for s in shapes]),
+        out_shape=[jax.ShapeDtypeStruct((2,) + s, BF) for s in shapes],
+        in_specs=[vmem] * 4,
+        out_specs=[pl.BlockSpec(memory_space=pltpu.HBM)] * 4,
+        scratch_shapes=landings
+        + [pltpu.VMEM((s[0], s[1] // 2), BF) for s in shapes]
+        + [dma((LANES, steps))] * 2
+        + [dma((count,))] * 7,
+        compiler_params=pltpu.CompilerParams(
+            collective_id=1, has_side_effects=True, vmem_limit_bytes=60 * 2**20
+        ),
+        name="scatter_gradients",
+    )(*grads)
+
+
+def dot(left, right):
+    return jnp.dot(left, right, preferred_element_type=F32)
+
+
+def dot_nt(left, right):
+    return lax.dot_general(left, right, (((1,), (1,)), ((), ())), preferred_element_type=F32)
+
+
+def dot_tn(left, right):
+    return lax.dot_general(left, right, (((0,), (0,)), ((), ())), preferred_element_type=F32)
+
+
+def rms_scale(values):
+    return lax.rsqrt(jnp.mean(values * values, axis=-1, keepdims=True) + EPSILON)
+
+
+def norm_backward(values, scale, gain, upstream):
+    weighted = gain * upstream
+    return scale * weighted - values * scale**3 * jnp.mean(values * weighted, axis=-1, keepdims=True)
+
+
+def swap_perm(n, kind):
+    out = []
+    for dp in range(4):
+        for f in range(n):
+            out.append((dp * n + f, (dp ^ kind) * n + f))
+    return out
+
+
+def valid_rows(item_lengths, frame_offsets):
+    slot = jnp.arange(ITEM_SLOTS)[None, None, :]
+    first = frame_offsets[:, :, None]
+    valid = (slot >= first) & (slot < first + item_lengths[:, :, None])
+    return valid.reshape(-1)
+
+
+def by_position(n, block_input, out_grad, item_lengths, frame_offsets, norm_attn, w_qkv, w_out, norm_ffn, w_gate_up, w_down):
+    x, c, f, r = place(n)
+    micro, frames, positions, width = block_input.shape
+    rows = micro * frames
+    hidden_size = w_gate_up.shape[2] // 2
+    head_dim = width // HEADS
+    valid = valid_rows(item_lengths, frame_offsets)[:, None]
+    inputs = block_input.reshape(rows, positions, width)
+    upstream = jnp.where(valid[..., None], out_grad.reshape(rows, positions, width), 0)
+
+    def take(array, at):
+        return lax.dynamic_index_in_dim(array, at, 1, keepdims=False)
+
+    rows_in, rows_up, all_qkv, all_out, all_gu, all_down = gather(
+        n, take(inputs, 1 - x), take(inputs, x), take(upstream, 1 - x), take(upstream, x), w_qkv, w_out, w_gate_up, w_down
+    )
+    gains = lax.all_gather(jnp.stack([norm_attn, norm_ffn]), "fsdp", axis=2, tiled=True)
+    gains = lax.dynamic_index_in_dim(gains, x, 1, keepdims=False).astype(F32)
+    gain_in, gain_two = gains[0][None], gains[1][None]
+    first = x == 0
+
+    def mate(array):
+        return lax.ppermute(array, AXES, swap_perm(n, 2))
+
+    def sib(array):
+        return lax.ppermute(array, AXES, swap_perm(n, 1))
+
+    values = rows_in.astype(F32)
+    scale_one = rms_scale(values)
+    normed = (values * scale_one * gain_in).astype(BF)
+    qkv = dot(normed, all_qkv).astype(BF)
+    query, key, value = qkv[:, :width], qkv[:, width : 2 * width], qkv[:, 2 * width :]
+    other = mate(qkv[:, width:])
+    key_o, value_o = other[:, :width], other[:, width:]
+    heads = (jnp.arange(width)[:, None] // head_dim == jnp.arange(HEADS)[None, :]).astype(F32)
+
+    def per_head(a, b):
+        return jnp.dot(a.astype(F32) * b.astype(F32), heads, precision=lax.Precision.HIGHEST)
+
+    def spread(p):
+        return jnp.dot(p, heads.T, precision=lax.Precision.HIGHEST)
+
+    score = per_head(query, key) / math.sqrt(head_dim)
+    score_o = jnp.where(first, -1e30, per_head(query, key_o) / math.sqrt(head_dim))
+    top = jnp.maximum(score, score_o)
+    ex, ex_o = jnp.exp(score - top), jnp.exp(score_o - top)
+    prob, prob_o = ex / (ex + ex_o), ex_o / (ex + ex_o)
+    low, low_o = spread(prob.astype(BF).astype(F32)), spread(prob_o.astype(BF).astype(F32))
+    mixed = (low * value.astype(F32) + low_o * value_o.astype(F32)).astype(BF)
+    middle = values + dot(mixed, all_out)
+    scale_two = rms_scale(middle)
+    normed_two = (middle * scale_two * gain_two).astype(BF)
+    gate_up = dot(normed_two, all_gu)
+    gate, up = gate_up[:, :hidden_size], gate_up[:, hidden_size:]
+    sigma = jax.nn.sigmoid(gate)
+    hidden = (gate * sigma * up).astype(BF)
+    output = (middle + dot(hidden, all_down)).astype(BF)
+
+    def halves(left, right):
+        cols = right.shape[1] // 2
+        theirs = lax.dynamic_slice_in_dim(right, (1 - c) * cols, cols, 1)
+        ours = lax.dynamic_slice_in_dim(right, c * cols, cols, 1)
+        return (dot_tn(left, ours) + sib(dot_tn(left, theirs).astype(BF)).astype(F32)).astype(BF)
+
+    grad_down = halves(hidden, rows_up)
+    grad_hidden = dot_nt(rows_up, all_down)
+    grad_gate = grad_hidden * up * sigma * (1.0 + gate * (1.0 - sigma))
+    grad_gu = jnp.concatenate([grad_gate, grad_hidden * gate * sigma], axis=-1).astype(BF)
+    grad_w_gu = halves(normed_two, grad_gu)
+    grad_normed_two = dot_nt(grad_gu, all_gu)
+    grad_gain_two = jnp.sum(grad_normed_two * middle * scale_two, axis=0)
+    grad_middle = rows_up.astype(F32) + norm_backward(middle, scale_two, gain_two, grad_normed_two)
+    grad_branch = grad_middle.astype(BF)
+    grad_w_out = halves(mixed, grad_branch)
+    grad_mixed = dot_nt(grad_branch, all_out).astype(BF)
+    gm = grad_mixed.astype(F32)
+    grad_prob = per_head(grad_mixed, value)
+    grad_prob_o = per_head(grad_mixed, value_o)
+    total = prob * grad_prob + prob_o * grad_prob_o
+    grad_score = spread(prob * (grad_prob - total) / math.sqrt(head_dim))
+    grad_score_o = spread(prob_o * (grad_prob_o - total) / math.sqrt(head_dim))
+    back = mate(jnp.concatenate([(grad_score_o * query.astype(F32)).astype(BF), (low_o * gm).astype(BF)], axis=-1))
+    back = jnp.where(first, back, 0).astype(F32)
+    grad_q = grad_score * key.astype(F32) + grad_score_o * key_o.astype(F32)
+    grad_k = grad_score * query.astype(F32) + back[:, :width]
+    grad_v = low * gm + back[:, width:]
+    grad_qkv = jnp.concatenate([grad_q, grad_k, grad_v], axis=-1).astype(BF)
+    grad_w_qkv = halves(normed, grad_qkv)
+    grad_normed = dot_nt(grad_qkv, all_qkv)
+    grad_gain_one = jnp.sum(grad_normed * values * scale_one, axis=0)
+    grad_in = (grad_middle + norm_backward(values, scale_one, gain_in, grad_normed)).astype(BF)
+
+    grads = scatter(n, [grad_w_qkv, grad_w_out, grad_w_gu, grad_down])
+    grads = [g.astype(F32) for g in grads]
+    gain_grads = jnp.stack([grad_gain_one, grad_gain_two])
+    gain_grads = jnp.stack([jnp.where(x == p, gain_grads, 0) for p in range(2)], axis=1)
+    gain_grads = lax.psum(gain_grads, AXES)
+    gain_grads = lax.dynamic_slice_in_dim(gain_grads, f * (width // n), width // n, 2)
+
+    def home(array):
+        ours = lax.dynamic_slice_in_dim(array, x * rows, rows, 0)
+        theirs = mate(lax.dynamic_slice_in_dim(array, (1 - x) * rows, rows, 0))
+        both = jnp.where(first, jnp.stack([ours, theirs], 1), jnp.stack([theirs, ours], 1))
+        return both.reshape(micro, frames, positions, width)
+
+    return home(output), home(grad_in), gain_grads[0], grads[0], grads[1], gain_grads[1], grads[2], grads[3]
 
 
 def shortened(x):
@@ -22,30 +418,11 @@
     return jax.tree.map(short, x)
 
 
-def rms_scale(values):
-    return lax.rsqrt(jnp.mean(values * values, axis=-1, keepdims=True) + EPSILON)
-
-
-def matmul(left, right):
-    return jnp.dot(left, right, preferred_element_type=jnp.float32)
-
-
-def contract_rows(left, right):
-    return jnp.einsum("fa,fb->ab", left, right, preferred_element_type=jnp.float32)
-
-
-def times_transposed(left, right):
-    return jnp.einsum("fb,ab->fa", left, right, preferred_element_type=jnp.float32)
-
-
-def norm_backward(values, scale, gain, upstream):
-    weighted = gain * upstream
-    return scale * weighted - values * scale**3 * jnp.mean(
-        values * weighted, axis=-1, keepdims=True
-    )
-
-
-def on_device(
+PRECISE = lax.Precision.HIGHEST
+matmul, times_transposed, contract_rows = dot, dot_nt, dot_tn
+
+
+def by_weights(
     block_input,
     out_grad,
     item_lengths,
@@ -59,7 +436,7 @@
 ):
     micro, frames, positions, model_width = block_input.shape
     head_dim = model_width // HEADS
-    hidden_size = FF
+    hidden_size = w_gate_up.shape[2] // 2
     head_shape = (frames, positions, HEADS, head_dim)
     slot_index = jnp.arange(ITEM_SLOTS)[None, None, :]
     first_slot = frame_offsets[:, :, None]
@@ -235,7 +612,18 @@
     )
 
 
+def fits(mesh, shapes):
+    return mesh.shape["dp"] == 4 and all(s[1] % 16 == 0 for s in shapes)
+
+
 def solution(mesh):
+    n = mesh.shape["fsdp"]
+
+    def on_device(*args):
+        if fits(mesh, [args[k].shape for k in (5, 6, 8, 9)]):
+            return by_position(n, *args)
+        return by_weights(*args)
+
     placed = (
         P(None, ("dp", "fsdp"), None, None),
         P(None, ("dp", "fsdp"), None, None),

time: 2920 us -> 815 us (0.28)
  waiting for transfers between devices: 2140 us -> 170 us
  Pallas kernels: 0 us -> 306 us
  matrix products: 428 us -> 187 us
  other arithmetic: 151 us -> 41.4 us
  local copies, waits for them, and re-layouts: 128 us -> 26.8 us
    reduce_scatter x4 -> x0, waiting for transfers between devices: 1250 us -> none  [the longest x1 728 us: on_device(): lax.psum_scatter(totals[4], 'fsdp', scatter_dimension=1, tiled=True)]
    all_gather x4 -> x0, waiting for transfers between devices: 664 us -> none  [the longest x1 378 us: on_device(): lax.all_gather(w_gate_up, 'fsdp', axis=1, tiled=True)]
    pallas_call x0 -> x2, Pallas kernels: none -> 306 us  [the longest x1 165 us: gather(): pl.pallas_call(functools.partial(gather_kernel, n, lanes, [s[0] for s in...]
    dot_general x58 -> x24, matrix products: 392 us -> 187 us  [the longest x4 59.1 us: dot_nt(): lax.dot_general(left, right, (((1,), (1,)), ((), ())), preferred_element_...]
    ppermute x0 -> x8, waiting for transfers between devices: none -> 170 us  [the longest x4 170 us: mate(): return lax.ppermute(array, AXES, swap_perm(n, 2))]
    psum x1 -> x0, waiting for transfers between devices: 117 us -> none  [on_device(): lax.psum(shortened(totals), 'dp')]
    unnamed x13 -> x0, waiting for transfers between devices: 106 us -> none
    add x8 -> x1, other arithmetic: 88.2 us -> 0.84 us  [valid_rows(): valid = (slot >= first) & (slot < first + item_lengths[:, :, None])]
  transfers between devices with their start and end apart: 11 -> 8, of which waited for: 9 -> 2; matrix products, arithmetic and copies ran while one was open for 20% -> 18% of each run, Pallas kernels for 0% -> 0%
where the time goes in v1:
time: 815 us; the launch traced here: 808 us
  Pallas kernels  306 us (38%)
  matrix products  187 us (23%)
  waiting for transfers between devices  170 us (21%)
  blocking collectives  71 us (9%)
  other arithmetic  41.4 us (5%)
  local copies, waits for them, and re-layouts  26.8 us (3%)
    ppermute x4, waiting for transfers between devices, mate(): return lax.ppermute(array, AXES, swap_perm(n, 2))  170 us
    pallas_call x1, Pallas kernels, gather(): pl.pallas_call(functools.partial(gather_kernel, n, lanes, [s[0] for s in...  165 us
    pallas_call x1, Pallas kernels, scatter(): pl.pallas_call(functools.partial(scatter_kernel, n, lanes, [s[0] for s in...  141 us
    dot_general x4, matrix products, dot_nt(): lax.dot_general(left, right, (((1,), (1,)), ((), ())), preferred_element_...  59.1 us
    dot_general x8, matrix products, dot_tn(): lax.dot_general(left, right, (((0,), (0,)), ((), ())), preferred_element_...  58.7 us
    psum x1, blocking collectives, by_position(): gain_grads = lax.psum(gain_grads, AXES)  48.5 us
    dot_general x4, matrix products, dot(): return jnp.dot(left, right, preferred_element_type=F32)  38.1 us
    all_gather x1, blocking collectives, by_position(): lax.all_gather(jnp.stack([norm_attn, norm_ffn]), 'fsdp', axis=2, tiled=True)  22.4 us
  transfers between devices with their start and end apart: 8, of which 2 were waited for; matrix products, arithmetic and copies ran while one was open for 18% of the time, Pallas kernels for 0%

profile of v1, /device:TPU:0, one launch (start us, length us, event | category | flops | bytes accessed | tf_op | source)
XLA Modules:
  0.0 808.0 jit_solution(7869435609840613570)
XLA Ops:
  4.4 4.3 constant_dynamic-slice_fusion.6
  12.3 164.6 %gather_weights.1 = (bf16[1024,1024]{1,0:T(8,128)(2,1)}, bf16[1024,1024]{1,0:T(8,128)(2,1)}, bf16[1024,3072]{1,0:T(8,128)(2,1)}, bf16[1024,1024]{1,0:T(8,128)(2,...) custom-call(bf16[512,1024]{1,0:T(8,128)(2,1)} %get-tuple-element.77.refs_0_, ...), custom_call_target="tpu_custom_call" | custom-call | tf_op jit(solution)/shard_map/gather_weights/pallas_call | solution.py:154
  179.6 22.4 %all_gather.3 = bf16[2,2,1024]{2,1,0:T(2,128)(2,1)S(1)} all-gather(bf16[2,2,128]{2,1,0:T(2,128)(2,1)S(1)} %pad_maximum_fusion.6), channel_id=1, replica_groups=mesh['dp'=4,'fsdp'=8] {'fsdp'}, dimensions={2}, use_global_device_ids=true | all-gather | bytes 9216 | tf_op jit(solution)/shard_map/all_gather | solution.py:321
  202.0 10.3 %convolution_convert_fusion = bf16[1024,3072]{1,0:T(8,128)(2,1)S(1)} fusion(bf16[1024,3072]{1,0:T(8,128)(2,1)} %get-tuple-element.19, bf16[1024,1024]{1,0:T(8,128)(2,1)} %get-tuple-element.18, f32[1024]{0:T(1024)S(1)} %bitcast.55, f32[1024]{0:T(1024)S(1)} %get-tuple-element.64), kind=kOutput, calls=%fused_computation.33 | convolution fusion | flops 6449790976 | bytes 14688256 | tf_op jit(solution)/shard_map/dot_general | solution.py:270
  217.9 4.6 fusion.47
  222.6 82.8 %collective-permute-done = bf16[1024,2048]{1,0:T(8,128)(2,1)} collective-permute-done((bf16[1024,2048]{1,0:T(8,128)(2,1)}, bf16[1024,2048]{1,0:T(8,128)(2,1)}, u32[]{:S(2)}, u32[]{:S(2)}) %collective-permute-start) | collective-permute-done | bytes 4194336 | tf_op jit(solution)/shard_map/ppermute | solution.py:327
  305.3 4.6 fusion.49
  310.8 6.1 fusion.15
  324.2 15.3 %fusion.109 = f32[1024,5632]{1,0:T(8,128)} fusion(bf16[1024,1024]{1,0:T(8,128)(2,1)S(1)} %multiply_convert_fusion.3, bf16[1024,5632]{1,0:T(8,128)(2,1)S(1)} %bitcast.65), kind=kOutput, calls=%fused_computation.178 | convolution fusion | flops 11811160064 | bytes 36700160 | tf_op jit(solution)/shard_map/dot_general | solution.py:270
  339.6 21.8 %multiply_convert_fusion.1 = (bf16[1024,2816]{1,0:T(8,128)(2,1)}, bf16[1024,2816]{1,0:T(8,128)(2,1)}, bf16[1024,2816]{1,0:T(8,128)(2,1)}) fusion(f32[1024,5632]{1,0:T(8,128)} %fusion.109, bf16[1024,1024]{1,0:T(8,128)(2,1)S(1)} %copy-done.13, bf16[2816,1024]{1,0:T(8,128)(2,1)} %get-tuple-element.22), kind=kOutput, calls=%fused_computation.8 | convolution fusion | flops 5951717376 | bytes 48234496 | tf_op jit(solution)/shard_map/dot_general | solution.py:274
  361.4 7.2 convolution_convert_fusion.1
  368.6 21.6 %multiply_reduce_fusion = (f32[1024]{0:T(1024)S(1)}, f32[1024]{0:T(1024)S(1)}, f32[1024,1024]{1,0:T(8,128)}) fusion(f32[1024,1024]{1,0:T(8,128)} %copy-done.1, f32[1024]{0:T(1024)S(1)} %get-tuple-element.66, f32[1024]{0:T(1024)S(1)} %bitcast.53, bf16[1024,5632]{1,0:T(8,128)(2,1)} %get-tuple-element.21, bf16[1024,2816]{1,0:T(8,128)(2,1)} %get-tuple-element.43, ...), kind=kOutput, calls=%fused_computation.64 | convolution fusion | flops 11840518144 | bytes 31473664 | tf_op jit(solution)/shard_map/dot_general | solution.py:274
  390.2 4.7 fusion.107
  395.6 3.8 fusion.23
  401.8 4.0 fusion.22
  407.8 6.2 fusion.13
  418.3 3.9 convolution_convert_fusion.4
  422.4 10.0 %add_convert_fusion.3 = bf16[1024,1024]{1,0:T(8,128)(2,1)S(1)} fusion(f32[1024,1024]{1,0:T(8,128)S(1)} %copy-done.2, bf16[1024,2816]{1,0:T(8,128)(2,1)} %get-tuple-element.44, bf16[2816,1024]{1,0:T(8,128)(2,1)} %get-tuple-element.22), kind=kOutput, calls=%fused_computation.68 | convolution fusion | flops 5907677184 | bytes 17825792 | tf_op jit(solution)/shard_map/dot_general | solution.py:270
  433.3 11.1 %fusion.7 = bf16[1024,2816]{1,0:T(8,128)(2,1)} fusion(bf16[1024,1024]{1,0:T(8,128)(2,1)} %copy-done.17, s32[]{:T(128)S(6)} %select_n.151, bf16[1024,2816]{1,0:T(8,128)(2,1)} %get-tuple-element.42, bf16[1024,2816]{1,0:T(8,128)(2,1)} %get-tuple-element.43), kind=kOutput, calls=%fused_computation.32 | convolution fusion | flops 5919997952 | bytes 19398660 | tf_op jit(solution)/shard_map/dot_general | solution.py:278
  444.6 87.6 %collective-permute-done.1 = bf16[512,1024]{1,0:T(8,128)(2,1)S(1)} collective-permute-done((bf16[512,1024]{1,0:T(8,128)(2,1)S(1)}, bf16[512,1024]{1,0:T(8,128)(2,1)S(1)}, u32[]{:S(2)}, u32[]{:S(2)}) %collective-permute-start.1) | collective-permute-done | bytes 1048608 | tf_op jit(solution)/shard_map/ppermute | solution.py:327
  532.6 3.5 copy.46
  536.1 3.5 add_convert_fusion.4.refs_1_
  542.3 5.8 fusion.19
  551.5 5.6 convolution_convert_fusion.2
  557.2 11.9 %fusion.35 = (f32[1024]{0:T(1024)S(1)}, f32[1024]{0:T(1024)S(1)}, f32[1024,1024]{1,0:T(8,128)}) fusion(bf16[1024,1024]{1,0:T(8,128)(2,1)S(1)} %copy-done.11, f32[1024]{0:T(1024)S(1)} %copy-done.25, f32[1024]{0:T(1024)S(1)} %bitcast.57, bf16[1024,3072]{1,0:T(8,128)(2,1)} %get-tuple-element.19, bf16[1024,1024]{1,0:T(8,128)(2,1)S(1)} %copy-done.9, ...), kind=kOutput, calls=%fused_computation.62 | convolution fusion | flops 6468663296 | bytes 18890752 | tf_op jit(solution)/shard_map/dot_general | solution.py:274
  573.9 7.6 add_convert_fusion.2.refs_3_
  581.6 48.5 %psum.7 = f32[2,2,1024]{2,1,0:T(2,128)S(1)} all-reduce(f32[2,2,1024]{2,1,0:T(2,128)S(1)} %pad_maximum_fusion.4), channel_id=1, replica_groups=mesh['dp'=4,'fsdp'=8] {'dp','fsdp'}, use_global_device_ids=true, to_apply=%region_6.7 | all-reduce | flops 4096 | bytes 32768 | tf_op jit(solution)/shard_map/psum | solution.py:401
  632.7 3.5 copy.47
  636.2 12.6 %add_convert_fusion.refs_2_ = bf16[1024,2816]{1,0:T(8,128)(2,1)} fusion(bf16[1024,2816]{1,0:T(8,128)(2,1)} %collective-permute-done.6, bf16[1024,1024]{1,0:T(8,128)(2,1)S(1)} %copy-done.18, s32[]{:T(128)S(6)} %select_n.150, bf16[1024,2816]{1,0:T(8,128)(2,1)} %get-tuple-element.42, bf16[1024,2816]{1,0:T(8,128)(2,1)} %get-tuple-element.43), kind=kOutput, calls=%fused_computation.6 | convolution fusion | flops 5925765120 | bytes 25165828 | tf_op jit(solution)/shard_map/dot_general | solution.py:278
  648.8 7.1 add_convert_fusion.1.refs_0_
  656.0 141.3 %scatter_gradients.1 = (bf16[2,128,3072]{2,1,0:T(8,128)(2,1)}, bf16[2,128,1024]{2,1,0:T(8,128)(2,1)}, bf16[2,128,5632]{2,1,0:T(8,128)(2,1)}, bf16[2,352,1024]{2,1,0:T(8,128)(2,1)}) custom-call(bf16[1024,1536]{1,0:T(8,128)(2,1)} %add_convert_fusion.1.refs_0_, bf16[1024,512]{1,0:T(8,128)(2,1)} %add_convert_fusion.4.refs_1_, ...), custom_call_target="tpu_custom_call" | custom-call | tf_op jit(solution)/shard_map/scatter_gradients/pallas_call | solution.py:253
  797.3 5.1 convert_element_type.176
  (132 shorter events, 53.3 us)
Async XLA Ops:
  12.3 167.2 %copy-start.29 = (bf16[2,128]{1,0:T(2,128)(2,1)S(1)}, bf16[2,128]{1,0:T(2,128)(2,1)}, u32[]{:S(2)}) copy-start(bf16[2,128]{1,0:T(2,128)(2,1)} %param.17) | copy-start | bytes 1540
  12.3 167.2 %copy-start.30 = (bf16[2,128]{1,0:T(2,128)(2,1)S(1)}, bf16[2,128]{1,0:T(2,128)(2,1)}, u32[]{:S(2)}) copy-start(bf16[2,128]{1,0:T(2,128)(2,1)} %param.14) | copy-start | bytes 1540
  179.6 32.8 %copy-start.24 = (f32[1024]{0:T(1024)}, f32[1024]{0:T(1024)S(1)}, u32[]{:S(2)}) copy-start(f32[1024]{0:T(1024)S(1)} %get-tuple-element.64) | copy-start | bytes 12292
  202.0 10.4 %copy-start.27 = (f32[1,1,1024]{2,1,0:T(1,128)}, f32[1,1,1024]{2,1,0:T(1,128)S(1)}, u32[]{:S(2)}) copy-start(f32[1,1,1024]{2,1,0:T(1,128)S(1)} %get-tuple-element.62) | copy-start | bytes 12292
  216.4 88.9 %collective-permute-start = (bf16[1024,2048]{1,0:T(8,128)(2,1)}, bf16[1024,2048]{1,0:T(8,128)(2,1)}, u32[]{:S(2)}, u32[]{:S(2)}) collective-permute-start(bf16[1024,2048]{1,0:T(8,128)(2,1)} %slice.61), channel_id=1, source_target_pairs={{0,16},{1,17},{2,18},{3,19},{4,20},{5,21},{6,22},{7,23},{8,24},{9,... | collective-permute-start | bytes 12582920 | tf_op jit(solution)/shard_map/ppermute | solution.py:327
  310.8 6.1 copy-start.3
  310.8 6.1 copy-start.10
  310.8 6.1 copy-start.31
  316.9 5.1 slice-start.4
  316.9 5.7 slice-start.5
  316.9 7.3 slice-start.6
  322.0 17.6 %copy-start.17 = (bf16[1024,1024]{1,0:T(8,128)(2,1)}, bf16[1024,1024]{1,0:T(8,128)(2,1)S(1)}, u32[]{:S(2)}) copy-start(bf16[1024,1024]{1,0:T(8,128)(2,1)S(1)} %multiply_convert_fusion.3) | copy-start | bytes 6291460
  324.2 15.3 %copy-start.13 = (bf16[1024,1024]{1,0:T(8,128)(2,1)S(1)}, bf16[1024,1024]{1,0:T(8,128)(2,1)}, u32[]{:S(2)}) copy-start(bf16[1024,1024]{1,0:T(8,128)(2,1)} %get-tuple-element.23) | copy-start | bytes 6291460
  368.6 204.5 %collective-permute-start.7 = (bf16[2816,512]{1,0:T(8,128)(2,1)}, bf16[2816,512]{1,0:T(8,128)(2,1)}, u32[]{:S(2)}, u32[]{:S(2)}) collective-permute-start(bf16[2816,512]{1,0:T(8,128)(2,1)} %convolution_convert_fusion.1), channel_id=1, source_target_pairs={{0,8},{1,9},{2,10},{3,11},{4,12},{5,13},{6,14},{7,15},{8,0},{9,1},... | collective-permute-start | bytes 8650760 | tf_op jit(solution)/shard_map/ppermute | solution.py:330
  390.2 5.3 copy-start.32
  390.2 9.1 %slice-start = ((s8[6291456]{0:T(1024)(128)(4,1)}), s8[4194304]{0:T(1024)(128)(4,1)S(1)}, s32[]{:S(2)}) async-start(s8[6291456]{0:T(1024)(128)(4,1)} %bitcast.43), calls=%async_computation | async-start | bytes 8388608
  414.0 134.1 %copy-start.6 = (bf16[1024,1024]{1,0:T(8,128)(2,1)}, bf16[1024,1024]{1,0:T(8,128)(2,1)S(1)}, u32[]{:S(2)}) copy-start(bf16[1024,1024]{1,0:T(8,128)(2,1)S(1)} %get-tuple-element.45) | copy-start | bytes 6291460
  416.8 5.6 copy-start.2
  416.8 122.8 %collective-permute-start.2 = (bf16[1024,2048]{1,0:T(8,128)(2,1)S(1)}, bf16[1024,2048]{1,0:T(8,128)(2,1)}, u32[]{:S(2)}, u32[]{:S(2)}) collective-permute-start(bf16[1024,2048]{1,0:T(8,128)(2,1)S(1)} %pad_maximum_fusion.3), channel_id=1, source_target_pairs={{0,16},{1,17},{2,18},{3,19},{4,20},{5,21},{6,22},{7,23},{8,24},{9,... | collective-permute-start | bytes 12582920 | tf_op jit(solution)/shard_map/ppermute | solution.py:327
  422.2 113.9 %collective-permute-start.5 = (bf16[1024,512]{1,0:T(8,128)(2,1)}, bf16[1024,512]{1,0:T(8,128)(2,1)}, u32[]{:S(2)}, u32[]{:S(2)}) collective-permute-start(bf16[1024,512]{1,0:T(8,128)(2,1)} %convolution_convert_fusion.4), channel_id=1, source_target_pairs={{0,8},{1,9},{2,10},{3,11},{4,12},{5,13},{6,14},{7,15},{8,0},{9,1},... | collective-permute-start | bytes 3145736 | tf_op jit(solution)/shard_map/ppermute | solution.py:330
  432.5 99.7 %collective-permute-start.1 = (bf16[512,1024]{1,0:T(8,128)(2,1)S(1)}, bf16[512,1024]{1,0:T(8,128)(2,1)S(1)}, u32[]{:S(2)}, u32[]{:S(2)}) collective-permute-start(bf16[512,1024]{1,0:T(8,128)(2,1)S(1)} %get-tuple-element.52), channel_id=1, source_target_pairs={{0,16},{1,17},{2,18},{3,19},{4,20},{5,21},{6,22},{7,23},{8,24},{9,... | collective-permute-start | bytes 3145736 | tf_op jit(solution)/shard_map/ppermute | solution.py:327
  444.5 191.7 %collective-permute-start.6 = (bf16[1024,2816]{1,0:T(8,128)(2,1)}, bf16[1024,2816]{1,0:T(8,128)(2,1)}, u32[]{:S(2)}, u32[]{:S(2)}) collective-permute-start(bf16[1024,2816]{1,0:T(8,128)(2,1)} %fusion.7), channel_id=1, source_target_pairs={{0,8},{1,9},{2,10},{3,11},{4,12},{5,13},{6,14},{7,15},{8,0},{9,1},... | collective-permute-start | bytes 17301512 | tf_op jit(solution)/shard_map/ppermute | solution.py:330
  551.5 5.7 copy-start.12
  551.5 5.7 copy-start.7
  551.5 5.7 copy-start.9
  557.1 11.9 %copy-start.26 = (f32[1024]{0:T(1024)S(1)}, f32[1024]{0:T(1024)}, u32[]{:S(2)}) copy-start(f32[1024]{0:T(1024)} %get-tuple-element.63) | copy-start | bytes 12292
  557.1 91.7 %collective-permute-start.4 = (bf16[1024,1536]{1,0:T(8,128)(2,1)}, bf16[1024,1536]{1,0:T(8,128)(2,1)}, u32[]{:S(2)}, u32[]{:S(2)}) collective-permute-start(bf16[1024,1536]{1,0:T(8,128)(2,1)} %convolution_convert_fusion.2), channel_id=1, source_target_pairs={{0,8},{1,9},{2,10},{3,11},{4,12},{5,13},{6,14},{7,15},{8,0},{9,1},... | collective-permute-start | bytes 9437192 | tf_op jit(solution)/shard_map/ppermute | solution.py:330
  573.1 57.6 %collective-permute-start.3 = (bf16[512,1024]{1,0:T(8,128)(2,1)}, bf16[512,1024]{1,0:T(8,128)(2,1)}, u32[]{:S(2)}, u32[]{:S(2)}) collective-permute-start(bf16[512,1024]{1,0:T(8,128)(2,1)} %get-tuple-element.50), channel_id=1, source_target_pairs={{0,16},{1,17},{2,18},{3,19},{4,20},{5,21},{6,22},{7,23},{8,24},{9,... | collective-permute-start | bytes 3145736 | tf_op jit(solution)/shard_map/ppermute | solution.py:327
  630.7 5.5 copy-start.18
  632.7 16.1 %slice-start.2 = ((s8[6291456]{0:T(1024)(128)(4,1)}), s8[4194304]{0:T(1024)(128)(4,1)S(1)}, s32[]{:S(2)}) async-start(s8[6291456]{0:T(1024)(128)(4,1)} %bitcast.46), calls=%async_computation.2 | async-start | bytes 8388608
  636.2 12.6 %slice-start.3 = ((s8[6291456]{0:T(1024)(128)(4,1)}), s8[2097152]{0:T(1024)(128)(4,1)S(1)}, s32[]{:S(2)}) async-start(s8[6291456]{0:T(1024)(128)(4,1)} %bitcast.46), calls=%async_computation.3 | async-start | bytes 4194304
  797.2 5.2 copy-start.21
  (16 other events, 54.9 us)
